TPU v7x, 32 devices: a whole 2x2x4 slice. The times are simulated.
32 devices in a mesh: dp: 8 (over z, y), head: 4 (over x, core).
Axes of the slice: x: 2, y: 2, z: 4, core: 2. Of those that a mesh axis runs over, the one named last changes fastest.
Arguments:
- tokens: bfloat16 [16, 1024, 512], P('dp', 'head'), may hold values from -6 to 6
- seq_counts: int32 [16], P('dp'), may hold values from 1 to 4, as said below
- seq_lengths: int32 [16, 4], P('dp'), may hold values from 0 to 1024, as said below
- query_key_value_weight: bfloat16 [2, 512, 1536], replicated, may hold values from -0.25 to 0.25
- output_weight: bfloat16 [2, 512, 512], replicated, may hold values from -3 to 3
- up_weight: bfloat16 [2, 512, 2048], replicated, may hold values from -0.25 to 0.25
- down_weight: bfloat16 [2, 2048, 512], replicated, may hold values from -0.125 to 0.125
- norm_gain: float32 [5, 512], replicated, may hold values from 0.5 to 1.5
- norm_bias: float32 [5, 512], replicated, may hold values from -1.5 to 1.5
- cotangent: bfloat16 [16, 1024, 512], P('dp', 'head'), may hold values from -6 to 6
Outputs:
- result: float32 [16, 1024, 512], P('dp', 'head')
- grad_tokens: float32 [16, 1024, 512], P('dp', 'head')
- grad_qkv: float32 [2, 512, 1536], P(None, 'dp')
- grad_out: float32 [2, 512, 512], P(None, 'dp')
- grad_up: float32 [2, 512, 2048], P(None, 'dp')
- grad_down: float32 [2, 2048, 512], P(None, 'dp')
- grad_gain: float32 [5, 512], P(None, 'dp')
- grad_bias: float32 [5, 512], P(None, 'dp')
Inputs may be any that keep to these rules, and one draw needn't show every extreme that they name: `seq_counts`: each entry is 1 or 4, the number of sequences in that slot of 1024 tokens; among the slots of one index of dp at least one holds a single sequence. `seq_lengths`: A slot with one sequence has its length in entry 0, from 512 to 1024, and zeros beside it; a slot with four has lengths of 1 to 256. Among the slots of one index of dp one holds a single sequence of 1024 tokens.
All inputs are finite; a program needn't handle non-finite values.
Results may differ from a plain program's by a relative error of at most 0.018.
Values may be sent and summed in bfloat16 or wider, within the bound.
A program may use at most 128 MiB of HBM per device.

v0:
```python
from functools import partial
import math

import jax
import jax.numpy as jnp
from jax import lax
from jax.sharding import PartitionSpec as P

HEADS = 8


EPS = 1e-05
NEG = -1e30


def norm_apply(values, gain_row, bias_row):
    centred = values - jnp.mean(values, axis=-1, keepdims=True)
    spread = jnp.mean(centred * centred, axis=-1, keepdims=True)
    return centred * lax.rsqrt(spread + EPS) * gain_row + bias_row


def smooth(values):
    return jax.nn.gelu(values, approximate=False)


def slot_masks(counts, lengths, full_len, quarter):
    positions = jnp.arange(full_len, dtype=jnp.int32)
    several = counts[:, None] == 4
    segment = jnp.where(several, positions[None, :] // quarter, 0)
    within = jnp.where(several, positions[None, :] % quarter, positions[None, :])
    choose = segment[:, :, None] == jnp.arange(4, dtype=jnp.int32)[None, None, :]
    limits = jnp.sum(jnp.where(choose, lengths[:, None, :], 0), axis=2)
    return (segment, within < limits)


def masked_scores(query_rows, key_rows, segment, usable, scaling):
    scores = (
        jnp.einsum("qhd,khd->hqk", query_rows, key_rows, preferred_element_type=jnp.float32)
        * scaling
    )
    allowed = (segment[:, None] == segment[None, :]) & usable[None, :]
    return jnp.where(allowed[None], scores, NEG)


def attend_forward(packet, scaling):
    packed_tokens, segment, usable = packet
    query_rows = packed_tokens[:, :, 0]
    key_rows = packed_tokens[:, :, 1]
    value_rows = packed_tokens[:, :, 2]
    scores = masked_scores(query_rows, key_rows, segment, usable, scaling)
    top_score = jnp.max(scores, axis=2, keepdims=True)
    row_total = jnp.sum(jnp.exp(scores - top_score), axis=2, keepdims=True)
    log_total = top_score + jnp.log(row_total)
    probs_low = jnp.exp(scores - log_total).astype(jnp.bfloat16)
    output = jnp.einsum("hqk,khd->qhd", probs_low, value_rows, preferred_element_type=jnp.float32)
    return (output.reshape(output.shape[0], -1), log_total[:, :, 0])


def attend_backward(packet, scaling):
    packed_tokens, grad_rows, log_total, segment, usable = packet
    query_rows = packed_tokens[:, :, 0]
    key_rows = packed_tokens[:, :, 1]
    value_rows = packed_tokens[:, :, 2]
    scores = masked_scores(query_rows, key_rows, segment, usable, scaling)
    probs_full = jnp.exp(scores - log_total[:, :, None])
    probs_low = probs_full.astype(jnp.bfloat16)
    grad_value = jnp.einsum(
        "hqk,qhd->khd", probs_low, grad_rows, preferred_element_type=jnp.float32
    )
    grad_probs = jnp.einsum(
        "qhd,khd->hqk", grad_rows, value_rows, preferred_element_type=jnp.float32
    )
    centre = jnp.sum(probs_full * grad_probs, axis=2, keepdims=True)
    grad_scores = (probs_full * (grad_probs - centre)).astype(jnp.bfloat16)
    grad_query = (
        jnp.einsum("hqk,khd->qhd", grad_scores, key_rows, preferred_element_type=jnp.float32)
        * scaling
    )
    grad_key = (
        jnp.einsum("hqk,qhd->khd", grad_scores, query_rows, preferred_element_type=jnp.float32)
        * scaling
    )
    return jnp.stack([grad_query, grad_key, grad_value], axis=2)


def body(
    tokens,
    seq_counts,
    seq_lengths,
    query_key_value_weight,
    output_weight,
    up_weight,
    down_weight,
    norm_gain,
    norm_bias,
    cotangent,
):
    groups = lax.axis_size("head")
    slot_count, local_len, model_width = tokens.shape
    full_len = local_len * groups
    layers = query_key_value_weight.shape[0]
    norms = norm_gain.shape[0]
    local_heads = HEADS // groups
    head_size = model_width // HEADS
    scaling = 1.0 / math.sqrt(head_size)
    segment, usable = slot_masks(seq_counts, seq_lengths, full_len, full_len // 4)
    normed = tokens.astype(jnp.float32)
    dual_sum = normed
    kept_attn = []
    kept_ffn = []
    for layer_index in range(layers):
        lowered_input = normed.astype(jnp.bfloat16)
        packed_tokens = jnp.einsum(
            "tog,gr->tor",
            lowered_input,
            query_key_value_weight[layer_index],
            preferred_element_type=jnp.float32,
        ).astype(jnp.bfloat16)
        head_view = lax.all_to_all(
            packed_tokens.reshape(slot_count, local_len, groups, -1),
            "head",
            split_axis=2,
            concat_axis=1,
            tiled=True,
        )
        head_view = head_view.reshape(slot_count, full_len, local_heads, 3, head_size)
        attended_rows, log_total = lax.map(
            partial(attend_forward, scaling=scaling), (head_view, segment, usable)
        )
        sequence_view = lax.all_to_all(
            attended_rows.astype(jnp.bfloat16).reshape(slot_count, full_len, 1, -1),
            "head",
            split_axis=1,
            concat_axis=2,
            tiled=True,
        )
        sequence_view = sequence_view.reshape(slot_count, local_len, model_width)
        branch_output = jnp.einsum(
            "mki,ib->mkb",
            sequence_view,
            output_weight[layer_index],
            preferred_element_type=jnp.float32,
        )
        dual_sum = dual_sum + branch_output
        pre_attn = normed + branch_output
        normed = norm_apply(pre_attn, norm_gain[2 * layer_index], norm_bias[2 * layer_index])
        kept_attn.append((lowered_input, head_view, log_total, sequence_view, pre_attn))
        lowered_middle = normed.astype(jnp.bfloat16)
        hidden_state = jnp.einsum(
            "irj,jc->irc",
            lowered_middle,
            up_weight[layer_index],
            preferred_element_type=jnp.float32,
        )
        active_tokens = smooth(hidden_state).astype(jnp.bfloat16)
        branch_output = jnp.einsum(
            "uqi,ip->uqp",
            active_tokens,
            down_weight[layer_index],
            preferred_element_type=jnp.float32,
        )
        dual_sum = dual_sum + branch_output
        pre_ffn = normed + branch_output
        normed = norm_apply(pre_ffn, norm_gain[2 * layer_index + 1], norm_bias[2 * layer_index + 1])
        kept_hidden = hidden_state
        kept_ffn.append((lowered_middle, kept_hidden, active_tokens, pre_ffn))
    final_out, final_pull = jax.vjp(
        norm_apply, dual_sum, norm_gain[norms - 1], norm_bias[norms - 1]
    )
    result = normed + final_out
    grad_normed = cotangent.astype(jnp.float32)
    grad_dual, last_gain, last_bias = final_pull(grad_normed)
    row_ids = jnp.arange(norms, dtype=jnp.int32)[:, None]
    qkv_list = [None] * layers
    out_list = [None] * layers
    up_list = [None] * layers
    down_list = [None] * layers
    gain_list = [None] * layers
    bias_list = [None] * layers
    for layer_index in reversed(range(layers)):
        gain_part = jnp.zeros((norms, model_width), jnp.float32)
        bias_part = jnp.zeros((norms, model_width), jnp.float32)
        if layer_index == layers - 1:
            gain_part = jnp.where(row_ids == norms - 1, last_gain[None, :], gain_part)
            bias_part = jnp.where(row_ids == norms - 1, last_bias[None, :], bias_part)
        lowered_middle, kept_hidden, active_tokens, pre_ffn = kept_ffn[layer_index]
        norm_row = 2 * layer_index + 1
        unused, norm_pull = jax.vjp(norm_apply, pre_ffn, norm_gain[norm_row], norm_bias[norm_row])
        grad_pre, grad_gain_row, grad_bias_row = norm_pull(grad_normed)
        gain_part = gain_part + jnp.where(row_ids == norm_row, grad_gain_row[None, :], 0.0)
        bias_part = bias_part + jnp.where(row_ids == norm_row, grad_bias_row[None, :], 0.0)
        branch_gradient = (grad_pre + grad_dual).astype(jnp.bfloat16)
        down_grad = jnp.einsum(
            "vpk,vpz->kz", active_tokens, branch_gradient, preferred_element_type=jnp.float32
        )
        grad_active = jnp.einsum(
            "rqj,wj->rqw",
            branch_gradient,
            down_weight[layer_index],
            preferred_element_type=jnp.float32,
        )
        hidden_state = kept_hidden
        unused, smooth_pull = jax.vjp(smooth, hidden_state)
        hidden_gradient = smooth_pull(grad_active)[0].astype(jnp.bfloat16)
        up_grad = jnp.einsum(
            "pxb,pxc->bc", lowered_middle, hidden_gradient, preferred_element_type=jnp.float32
        )
        grad_normed = grad_pre + jnp.einsum(
            "jte,ae->jta",
            hidden_gradient,
            up_weight[layer_index],
            preferred_element_type=jnp.float32,
        )
        lowered_input, head_view, log_total, sequence_view, pre_attn = kept_attn[layer_index]
        norm_row = 2 * layer_index
        unused, norm_pull = jax.vjp(norm_apply, pre_attn, norm_gain[norm_row], norm_bias[norm_row])
        grad_pre, grad_gain_row, grad_bias_row = norm_pull(grad_normed)
        gain_part = gain_part + jnp.where(row_ids == norm_row, grad_gain_row[None, :], 0.0)
        bias_part = bias_part + jnp.where(row_ids == norm_row, grad_bias_row[None, :], 0.0)
        branch_gradient = (grad_pre + grad_dual).astype(jnp.bfloat16)
        out_grad = jnp.einsum(
            "uwb,uwg->bg", sequence_view, branch_gradient, preferred_element_type=jnp.float32
        )
        grad_attended = jnp.einsum(
            "xom,cm->xoc",
            branch_gradient,
            output_weight[layer_index],
            preferred_element_type=jnp.float32,
        ).astype(jnp.bfloat16)
        grad_heads = lax.all_to_all(
            grad_attended.reshape(slot_count, local_len, groups, -1),
            "head",
            split_axis=2,
            concat_axis=1,
            tiled=True,
        )
        grad_heads = grad_heads.reshape(slot_count, full_len, local_heads, head_size)
        grad_packed = lax.map(
            partial(attend_backward, scaling=scaling),
            (head_view, grad_heads, log_total, segment, usable),
        )
        grad_packed = grad_packed.astype(jnp.bfloat16).reshape(slot_count, full_len, 1, -1)
        sequence_gradient = lax.all_to_all(
            grad_packed, "head", split_axis=1, concat_axis=2, tiled=True
        )
        sequence_gradient = sequence_gradient.reshape(slot_count, local_len, 3 * model_width)
        query_key_value_gradient = jnp.einsum(
            "xwz,xwu->zu", lowered_input, sequence_gradient, preferred_element_type=jnp.float32
        )
        grad_normed = grad_pre + jnp.einsum(
            "mki,ti->mkt",
            sequence_gradient,
            query_key_value_weight[layer_index],
            preferred_element_type=jnp.float32,
        )
        qkv_list[layer_index] = query_key_value_gradient
        out_list[layer_index] = out_grad
        up_list[layer_index] = up_grad
        down_list[layer_index] = down_grad
        gain_list[layer_index] = gain_part
        bias_list[layer_index] = bias_part
    grad_tokens = grad_normed + grad_dual
    gain_total = sum(gain_list[1:], gain_list[0])
    bias_total = sum(bias_list[1:], bias_list[0])
    summed = (
        lax.psum_scatter(jnp.stack(qkv_list), "dp", scatter_dimension=1, tiled=True),
        lax.psum_scatter(jnp.stack(out_list), "dp", scatter_dimension=1, tiled=True),
        lax.psum_scatter(jnp.stack(up_list), "dp", scatter_dimension=1, tiled=True),
        lax.psum_scatter(jnp.stack(down_list), "dp", scatter_dimension=1, tiled=True),
        lax.psum_scatter(gain_total, "dp", scatter_dimension=1, tiled=True),
        lax.psum_scatter(bias_total, "dp", scatter_dimension=1, tiled=True),
    )
    summed = (
        lax.psum(summed[0].astype(jnp.bfloat16), "head").astype(jnp.float32),
        lax.psum(summed[1].astype(jnp.bfloat16), "head").astype(jnp.float32),
        lax.psum(summed[2].astype(jnp.bfloat16), "head").astype(jnp.float32),
        lax.psum(summed[3].astype(jnp.bfloat16), "head").astype(jnp.float32),
        lax.psum(summed[4].astype(jnp.bfloat16), "head").astype(jnp.float32),
        lax.psum(summed[5].astype(jnp.bfloat16), "head").astype(jnp.float32),
    )
    grad_qkv, grad_out, grad_up, grad_down, grad_gain, grad_bias = summed
    return (result, grad_tokens, grad_qkv, grad_out, grad_up, grad_down, grad_gain, grad_bias)


def solution(mesh):
    return jax.shard_map(
        body,
        mesh=mesh,
        in_specs=(
            P("dp", "head", None),
            P("dp"),
            P("dp", None),
            P(),
            P(),
            P(),
            P(),
            P(),
            P(),
            P("dp", "head", None),
        ),
        out_specs=(
            P("dp", "head", None),
            P("dp", "head", None),
            P(None, "dp", None),
            P(None, "dp", None),
            P(None, "dp", None),
            P(None, "dp", None),
            P(None, "dp"),
            P(None, "dp"),
        ),
        check_vma=False,
    )
```

profile of v0, /device:TPU:0, one launch (start us, length us, event | category | flops | bytes accessed | tf_op | source)
XLA Modules:
  0.0 1045.8 jit_solution(6715123418046075589)
XLA Ops:
  7.2 2.6 convolution_convert_fusion.1
  10.2 2.6 copy.166
  12.7 4.2 all-to-all-start
  17.2 19.8 %all-to-all-done = bf16[2,256,4,384]{1,3,0,2:T(8,128)(2,1)S(1)} async-done(((bf16[2,256,4,384]{1,3,0,2:T(8,128)(2,1)}), bf16[2,256,4,384]{1,3,0,2:T(8,128)(2,1)S(1)}, u32[]{:S(2)}, u32[]{:S(2)}) %all-to-all-start) | async-done | bytes 1572896 | tf_op jit(solution)/shard_map/all_to_all | solution.py:119
  43.2 41.6 %while.44 = (s32[]{:T(128)}, bf16[2,1024,128]{2,0,1:T(2,128)(2,1)}, f32[2,2,1024]{2,1,0:T(2,128)S(1)}, bf16[2,1024,2,3,64]{1,4,2,3,0:T(8,128)(2,1)S(1)}, s32[2,1...) while((s32[]{:T(128)}, bf16[2,1024,128]{2,0,1:T(2,128)(2,1)}, ...), condition=%wide.region_4.5_spmd, body=%wide.region_1.4_spmd.sunk | while | flops 562034688 | bytes 33111144 | solution.py:127
  51.1 12.9 %dynamic_update_slice.32 = bf16[2,1024,128]{2,0,1:T(2,128)(2,1)} dynamic-update-slice(bf16[2,1024,128]{2,0,1:T(2,128)(2,1)} %get-tuple-element.639, bf16[1,1024,128]{2,0,1:T(2,128)(2,1)S(1)} %copy.276, s32[]{:T(128)} %get-tuple-element.638, s32[]{:T(128)} %constant.171.clone.1..sunk, s32[]{:T(128)} %constant.171.clone.1..sunk) | dynamic-update-slice | bytes 524292 | tf_op jit(solution)/shard_map/while/body/jit(dynamic_update_index_in_dim)/dynamic_update_slice | solution.py:127
  71.9 12.9 %dynamic_update_slice.32 = bf16[2,1024,128]{2,0,1:T(2,128)(2,1)} dynamic-update-slice(bf16[2,1024,128]{2,0,1:T(2,128)(2,1)} %get-tuple-element.639, bf16[1,1024,128]{2,0,1:T(2,128)(2,1)S(1)} %copy.276, s32[]{:T(128)} %get-tuple-element.638, s32[]{:T(128)} %constant.171.clone.1..sunk, s32[]{:T(128)} %constant.171.clone.1..sunk) | dynamic-update-slice | bytes 524292 | tf_op jit(solution)/shard_map/while/body/jit(dynamic_update_index_in_dim)/dynamic_update_slice | solution.py:127
  84.8 3.6 all-to-all-start.1
  88.5 8.7 all-to-all-done.1
  100.1 4.1 fusion.121
  104.3 10.5 %multiply_convert_fusion.3 = (bf16[2,256,2048]{2,1,0:T(8,128)(2,1)S(1)}, f32[2,256,2048]{2,1,0:T(8,128)}) fusion(f32[2,256,2048]{2,1,0:T(8,128)S(1)} %get-tuple-element.433, u8[256,2048]{1,0:T(8,128)(4,1)S(1)} %get-tuple-element.301, u8[256,2048]{1,0:T(8,128)(4,1)S(1)} %get-tuple-element.300), kind=kLoop, calls=%fused_computation.129 | loop fusion | flops 73400320 | bytes 11534336 | tf_op jit(solution)/shard_map/convert_element_type | solution.py:155
  120.1 3.9 reshape.612
  124.0 3.8 copy.171
  127.8 3.8 all-to-all-start.2
  131.6 20.0 %all-to-all-done.2 = bf16[2,256,4,384]{1,3,0,2:T(8,128)(2,1)S(1)} async-done(((bf16[2,256,4,384]{1,3,0,2:T(8,128)(2,1)}), bf16[2,256,4,384]{1,3,0,2:T(8,128)(2,1)S(1)}, u32[]{:S(2)}, u32[]{:S(2)}) %all-to-all-start.2) | async-done | bytes 1572896 | tf_op jit(solution)/shard_map/all_to_all | solution.py:119
  154.0 3.8 reshape.613
  160.4 41.6 %while.45 = (s32[]{:T(128)}, bf16[2,1024,128]{2,0,1:T(2,128)(2,1)}, f32[2,2,1024]{2,1,0:T(2,128)S(1)}, bf16[2,1024,2,3,64]{1,4,2,3,0:T(8,128)(2,1)S(1)}, s32[2,1...) while((s32[]{:T(128)}, bf16[2,1024,128]{2,0,1:T(2,128)(2,1)}, ...), condition=%wide.region_12.13_spmd, body=%wide.region_9.12_spmd.sunk | while | flops 562034688 | bytes 33111144 | solution.py:127
  165.5 2.5 fusion.226
  168.3 12.9 %dynamic_update_slice.34 = bf16[2,1024,128]{2,0,1:T(2,128)(2,1)} dynamic-update-slice(bf16[2,1024,128]{2,0,1:T(2,128)(2,1)} %get-tuple-element.663, bf16[1,1024,128]{2,0,1:T(2,128)(2,1)S(1)} %copy.277, s32[]{:T(128)} %get-tuple-element.662, s32[]{:T(128)} %constant.171.clone.1..sunk.1, s32[]{:T(128)} %constant.171.clone.1..sunk.1) | dynamic-update-slice | bytes 524292 | tf_op jit(solution)/shard_map/while/body/jit(dynamic_update_index_in_dim)/dynamic_update_slice | solution.py:127
  186.3 2.5 fusion.226
  189.1 12.9 %dynamic_update_slice.34 = bf16[2,1024,128]{2,0,1:T(2,128)(2,1)} dynamic-update-slice(bf16[2,1024,128]{2,0,1:T(2,128)(2,1)} %get-tuple-element.663, bf16[1,1024,128]{2,0,1:T(2,128)(2,1)S(1)} %copy.277, s32[]{:T(128)} %get-tuple-element.662, s32[]{:T(128)} %constant.171.clone.1..sunk.1, s32[]{:T(128)} %constant.171.clone.1..sunk.1) | dynamic-update-slice | bytes 524292 | tf_op jit(solution)/shard_map/while/body/jit(dynamic_update_index_in_dim)/dynamic_update_slice | solution.py:127
  202.0 12.7 %all_to_all.120 = bf16[2,1024,1,128]{3,0,2,1:T(2,128)(2,1)S(1)} all-to-all(bf16[2,1024,1,128]{3,0,2,1:T(2,128)(2,1)} %bitcast.430), channel_id=1, replica_groups=mesh['dp'=8,'head'=4] {'head'}, dimensions={1} | all-to-all | bytes 1048576 | tf_op jit(solution)/shard_map/all_to_all | solution.py:130
  222.4 9.6 multiply_convert_fusion.2
  238.7 2.5 add_convert_fusion.1
  247.3 3.6 all-to-all-start.4
  251.0 8.8 all-to-all-done.4
  263.6 27.6 %while.46 = (s32[]{:T(128)}, bf16[2,1024,2,3,64]{1,4,3,2,0:T(8,128)(2,1)}, bf16[2,1024,2,3,64]{1,4,2,3,0:T(8,128)(2,1)S(1)}, s32[2,1024]{1,0:T(2,128)S(1)}, pred...) while((s32[]{:T(128)}, ...), condition=%wide.region_27.28_spmd, body=%wide.region_25.27_spmd.sunk | while | flops 1377040384 | bytes 72949352 | solution.py:238
  266.0 3.0 multiply_reduce_fusion.15
  269.0 2.7 multiply_convert_fusion.6
  274.0 2.5 fusion.232
  279.8 3.0 multiply_reduce_fusion.15
  282.8 2.7 multiply_convert_fusion.6
  287.8 2.5 fusion.232
  291.2 5.1 copy.180
  296.3 4.3 all-to-all-start.5
  302.6 18.2 %all-to-all-done.5 = bf16[2,1024,1,384]{3,0,2,1:T(2,128)(2,1)} async-done(((bf16[2,1024,1,384]{3,0,2,1:T(2,128)(2,1)}), bf16[2,1024,1,384]{3,0,2,1:T(2,128)(2,1)}, u32[]{:S(2)}, u32[]{:S(2)}) %all-to-all-start.5) | async-done | bytes 1572896 | tf_op jit(solution)/shard_map/all_to_all | solution.py:243
  324.8 3.8 reshape.619
  328.6 3.6 multiply_reduce_fusion.4
  334.8 2.5 add_convert_fusion
  343.4 3.0 convolution_bitcast_fusion
  347.8 4.2 pad_maximum_fusion.1
  353.2 3.2 convolution_bitcast_fusion.2
  357.8 3.8 pad_maximum_fusion
  363.6 11.2 %all_to_all.121 = bf16[2,256,4,128]{3,1,0,2:T(8,128)(2,1)S(1)} all-to-all(bf16[2,256,4,128]{3,1,0,2:T(8,128)(2,1)S(1)} %bitcast.435), channel_id=1, replica_groups=mesh['dp'=8,'head'=4] {'head'}, dimensions={2} | all-to-all | bytes 1048576 | tf_op jit(solution)/shard_map/all_to_all | solution.py:230
  376.9 27.6 %while.47 = (s32[]{:T(128)}, bf16[2,1024,2,3,64]{1,4,3,2,0:T(8,128)(2,1)}, bf16[2,1024,2,3,64]{1,4,2,3,0:T(8,128)(2,1)S(1)}, s32[2,1024]{1,0:T(2,128)S(1)}, pred...) while((s32[]{:T(128)}, ...), condition=%wide.region_34.35_spmd, body=%wide.region_32.34_spmd.sunk | while | flops 1377040384 | bytes 72949352 | solution.py:238
  379.3 3.0 multiply_reduce_fusion.16
  382.3 2.7 multiply_convert_fusion.7
  387.3 2.5 fusion.240
  393.1 3.0 multiply_reduce_fusion.16
  396.1 2.7 multiply_convert_fusion.7
  401.1 2.5 fusion.240
  404.6 5.1 copy.187
  409.7 3.6 all-to-all-start.7
  416.8 4.2 convolution_bitcast_fusion.4
  421.0 12.3 %all-to-all-done.7 = bf16[2,1024,1,384]{3,0,2,1:T(2,128)(2,1)S(1)} async-done(((bf16[2,1024,1,384]{3,0,2,1:T(2,128)(2,1)}), bf16[2,1024,1,384]{3,0,2,1:T(2,128)(2,1)S(1)}, u32[]{:S(2)}, u32[]{:S(2)}) %all-to-all-start.7) | async-done | bytes 1572896 | tf_op jit(solution)/shard_map/all_to_all | solution.py:243
  437.6 3.4 pad_maximum_fusion.2
  441.0 10.5 %copy.193 = f32[2,512,1536]{2,0,1:T(2,128)} copy(f32[2,512,1536]{1,2,0:T(8,128)} %pad_maximum_fusion.2) | data formatting | bytes 12582912 | tf_op jit(solution)/shard_map/stack | solution.py:266
  451.4 302.6 %all-reduce.7 = bf16[2,512,1536]{2,0,1:T(2,128)(2,1)} all-reduce(f32[2,512,1536]{2,0,1:T(2,128)} %copy.193), channel_id=2, replica_groups=mesh['dp'=8,'head'=4] {'dp'}, use_global_device_ids=true, to_apply=%region_35.36.clone | all-reduce | flops 1572864 | bytes 9437184
  759.8 98.4 %reduce-scatter.12.cloned.1.call-done = f32[2,64,2048]{2,1,0:T(8,128)} async-done(((f32[2,512,2048]{2,1,0:T(8,128)}), f32[2,64,2048]{2,1,0:T(8,128)}) %reduce-scatter.12.cloned.1.call-update) | async-done | bytes 1048592 | tf_op jit(solution)/shard_map/reduce_scatter | solution.py:268
  860.4 61.9 %reduce-scatter.16.cloned.1.call-done = f32[64,5]{1,0:T(8,128)} async-done(((f32[512,5]{1,0:T(8,128)}), f32[64,5]{1,0:T(8,128)}) %reduce-scatter.16.cloned.1.call-update) | async-done | bytes 1296
  923.1 63.2 %reduce-scatter.18.cloned.1.call-done = f32[64,5]{1,0:T(8,128)} async-done(((f32[512,5]{1,0:T(8,128)}), f32[64,5]{1,0:T(8,128)}) %reduce-scatter.18.cloned.1.call-update) | async-done | bytes 1296
  987.1 5.6 all-reduce.1
  993.9 3.7 fusion.100
  997.7 34.1 %all-reduce.6.cloned.1.call-done = (bf16[2,64,1536]{2,0,1:T(2,128)(2,1)}, bf16[2,64,512]{2,1,0:T(8,128)(2,1)}, bf16[2,64,2048]{2,1,0:T(8,128)(2,1)}, bf16[2,256,512]{2,1,0:T(8,128)(2,1)}) async-done(((bf16[2,64,1536]{2,0,1:T(2,128)(2,1)}, bf16[2,64,512]{2,1,0:T(8,128)(2,1)}, bf16[2,64,2048]{2,1,0:T(8,128)(2,1)}, bf16[2,256,512]{2,1,0:T(8,128)(2,1)}), (bf16[2,64,1536]{2,0,1:T(2,128)(2,1)}, ...) | async-done | bytes 1572880 | tf_op jit(solution)/shard_map/psum | solution.py:274
  (339 shorter events, 140.1 us)
Async XLA Ops:
  9.7 7.2 copy-start.75
  9.7 7.3 copy-start.71
  12.7 24.3 %all-to-all-start = ((bf16[2,256,4,384]{1,3,0,2:T(8,128)(2,1)}), bf16[2,256,4,384]{1,3,0,2:T(8,128)(2,1)S(1)}, u32[]{:S(2)}, u32[]{:S(2)}) async-start(bf16[2,256,4,384]{1,3,0,2:T(8,128)(2,1)} %copy.166), calls=%async_computation | async-start | bytes 3145728 | tf_op jit(solution)/shard_map/all_to_all | solution.py:119
  43.2 45.3 %copy-start.67 = (f32[5,512]{1,0:T(8,128)S(1)}, f32[5,512]{1,0:T(8,128)}, u32[]{:S(2)}) copy-start(f32[5,512]{1,0:T(8,128)} %param.25) | copy-start | bytes 30724
  43.2 45.3 %copy-start.68 = (f32[5,512]{1,0:T(8,128)S(1)}, f32[5,512]{1,0:T(8,128)}, u32[]{:S(2)}) copy-start(f32[5,512]{1,0:T(8,128)} %param.26) | copy-start | bytes 30724
  84.8 12.5 %copy-start.41 = (f32[2,2,1024]{2,1,0:T(2,128)}, f32[2,2,1024]{2,1,0:T(2,128)S(1)}, u32[]{:S(2)}) copy-start(f32[2,2,1024]{2,1,0:T(2,128)S(1)} %get-tuple-element.707) | copy-start | bytes 49156
  84.8 19.4 %copy-start = (bf16[2,1024,2,3,64]{1,4,2,3,0:T(8,128)(2,1)}, bf16[2,1024,2,3,64]{1,4,2,3,0:T(8,128)(2,1)S(1)}, u32[]{:S(2)}) copy-start(bf16[2,1024,2,3,64]{1,4,2,3,0:T(8,128)(2,1)S(1)} %get-tuple-element.739) | copy-start | bytes 4718596
  84.8 12.4 %all-to-all-start.1 = ((bf16[2,1024,1,128]{3,0,2,1:T(2,128)(2,1)}), bf16[2,1024,1,128]{3,0,2,1:T(2,128)(2,1)S(1)}, u32[]{:S(2)}, u32[]{:S(2)}) async-start(bf16[2,1024,1,128]{3,0,2,1:T(2,128)(2,1)} %bitcast.259), calls=%async_computation.1 | async-start | bytes 1048576 | tf_op jit(solution)/shard_map/all_to_all | solution.py:130
  88.5 26.3 %copy-start.46 = (f32[1,512]{1,0:T(1,128)}, f32[1,512]{1,0:T(1,128)S(1)}, u32[]{:S(2)}) copy-start(f32[1,512]{1,0:T(1,128)S(1)} %get-tuple-element.420) | copy-start | bytes 6148
  88.5 26.3 %copy-start.52 = (f32[1,512]{1,0:T(1,128)}, f32[1,512]{1,0:T(1,128)S(1)}, u32[]{:S(2)}) copy-start(f32[1,512]{1,0:T(1,128)S(1)} %get-tuple-element.425) | copy-start | bytes 6148
  88.5 128.6 %copy-start.60 = (f32[1,512]{1,0:T(1,128)}, f32[1,512]{1,0:T(1,128)S(1)}, u32[]{:S(2)}) copy-start(f32[1,512]{1,0:T(1,128)S(1)} %get-tuple-element.424) | copy-start | bytes 6148
  88.5 143.5 %copy-start.44 = (f32[1,512]{1,0:T(1,128)}, f32[1,512]{1,0:T(1,128)S(1)}, u32[]{:S(2)}) copy-start(f32[1,512]{1,0:T(1,128)S(1)} %get-tuple-element.423) | copy-start | bytes 6148
  97.8 6.4 copy-start.14
  99.8 132.3 %copy-start.4 = (f32[2,256,512]{2,1,0:T(8,128)}, f32[2,256,512]{2,1,0:T(8,128)S(1)}, u32[]{:S(2)}) copy-start(f32[2,256,512]{2,1,0:T(8,128)S(1)} %get-tuple-element.432) | copy-start | bytes 3145732
  99.8 15.0 %copy-start.50 = (f32[2,256]{1,0:T(2,128)}, f32[2,256]{1,0:T(2,128)S(1)}, u32[]{:S(2)}) copy-start(f32[2,256]{1,0:T(2,128)S(1)} %broadcast_multiply_fusion.4) | copy-start | bytes 6148
  100.1 4.2 copy-start.56
  100.1 14.7 %copy-start.54 = (f32[2,256]{1,0:T(2,128)}, f32[2,256]{1,0:T(2,128)S(1)}, u32[]{:S(2)}) copy-start(f32[2,256]{1,0:T(2,128)S(1)} %fusion.151) | copy-start | bytes 6148
  104.2 10.5 %copy-start.22 = (f32[2,256,2048]{2,1,0:T(8,128)}, f32[2,256,2048]{2,1,0:T(8,128)S(1)}, u32[]{:S(2)}) copy-start(f32[2,256,2048]{2,1,0:T(8,128)S(1)} %get-tuple-element.433) | copy-start | bytes 12582916
  104.3 10.5 %copy-start.35 = (bf16[2,2048,512]{2,1,0:T(8,128)(2,1)S(1)}, bf16[2,2048,512]{2,1,0:T(8,128)(2,1)}, u32[]{:S(2)}) copy-start(bf16[2,2048,512]{2,1,0:T(8,128)(2,1)} %param.24) | copy-start | bytes 12582916
  114.8 3.0 copy-start.74
  117.1 6.9 copy-start.11
  117.4 6.6 copy-start.58
  127.8 23.8 %all-to-all-start.2 = ((bf16[2,256,4,384]{1,3,0,2:T(8,128)(2,1)}), bf16[2,256,4,384]{1,3,0,2:T(8,128)(2,1)S(1)}, u32[]{:S(2)}, u32[]{:S(2)}) async-start(bf16[2,256,4,384]{1,3,0,2:T(8,128)(2,1)} %copy.171), calls=%async_computation.2 | async-start | bytes 3145728 | tf_op jit(solution)/shard_map/all_to_all | solution.py:119
  217.1 5.3 copy-start.17
  217.1 2.9 copy-start.72
  219.3 24.1 %copy-start.6 = (f32[2,256,512]{2,1,0:T(8,128)}, f32[2,256,512]{2,1,0:T(8,128)S(1)}, u32[]{:S(2)}) copy-start(f32[2,256,512]{2,1,0:T(8,128)S(1)} %get-tuple-element.398) | copy-start | bytes 3145732
  222.4 9.6 copy-start.36
  222.4 9.6 copy-start.38
  237.0 102.5 %copy-start.2 = (f32[2,256,512]{2,1,0:T(8,128)}, f32[2,256,512]{2,1,0:T(8,128)S(1)}, u32[]{:S(2)}) copy-start(f32[2,256,512]{2,1,0:T(8,128)S(1)} %get-tuple-element.416) | copy-start | bytes 3145732
  237.0 102.5 %copy-start.48 = (f32[2,256]{1,0:T(2,128)}, f32[2,256]{1,0:T(2,128)S(1)}, u32[]{:S(2)}) copy-start(f32[2,256]{1,0:T(2,128)S(1)} %negate_multiply_fusion.5) | copy-start | bytes 6148
  247.3 12.5 %all-to-all-start.4 = ((bf16[2,256,4,128]{3,1,0,2:T(8,128)(2,1)}), bf16[2,256,4,128]{3,1,0,2:T(8,128)(2,1)S(1)}, u32[]{:S(2)}, u32[]{:S(2)}) async-start(bf16[2,256,4,128]{3,1,0,2:T(8,128)(2,1)} %bitcast.431), calls=%async_computation.4 | async-start | bytes 1048576 | tf_op jit(solution)/shard_map/all_to_all | solution.py:230
  291.2 9.9 copy-start.18
  291.2 9.9 copy-start.27
  296.3 24.5 %all-to-all-start.5 = ((bf16[2,1024,1,384]{3,0,2,1:T(2,128)(2,1)}), bf16[2,1024,1,384]{3,0,2,1:T(2,128)(2,1)}, u32[]{:S(2)}, u32[]{:S(2)}) async-start(bf16[2,1024,1,384]{3,0,2,1:T(2,128)(2,1)} %copy.180), calls=%async_computation.5 | async-start | bytes 3145728 | tf_op jit(solution)/shard_map/all_to_all | solution.py:243
  300.6 455.5 %reduce-scatter.10.cloned.1.call-start = ((), (), s32[]{:S(2)}) async-start(), calls=%async_computation.13 | async-start | bytes 2359296 | tf_op jit(solution)/shard_map/reduce_scatter | solution.py:267
  302.6 26.0 %copy-start.12 = (f32[2,256,512]{2,1,0:T(8,128)S(1)}, f32[2,256,512]{2,1,0:T(8,128)}, u32[]{:S(2)}) copy-start(f32[2,256,512]{2,1,0:T(8,128)} %copy-done.11) | copy-start | bytes 3145732
  322.4 9.9 copy-start.59
  328.6 4.4 copy-start.24
  328.6 4.7 copy-start.37
  339.0 2.7 copy-start.21
  339.5 3.8 copy-start.62
  343.3 414.4 %reduce-scatter.14.cloned.1.call-start = ((), (), s32[]{:S(2)}) async-start(), calls=%async_computation.15 | async-start | bytes 9437184 | tf_op jit(solution)/shard_map/reduce_scatter | solution.py:269
  343.4 3.1 copy-start.10
  352.0 4.4 copy-start.53
  352.0 506.2 %reduce-scatter.12.cloned.1.call-start = ((), (), s32[]{:S(2)}) async-start(), calls=%async_computation.14 | async-start | bytes 9437184 | tf_op jit(solution)/shard_map/reduce_scatter | solution.py:268
  353.2 3.2 copy-start.32
  363.0 13.8 %copy-start.1 = (bf16[2,1024,2,3,64]{1,4,2,3,0:T(8,128)(2,1)S(1)}, bf16[2,1024,2,3,64]{1,4,2,3,0:T(8,128)(2,1)}, u32[]{:S(2)}) copy-start(bf16[2,1024,2,3,64]{1,4,2,3,0:T(8,128)(2,1)} %copy-done) | copy-start | bytes 4718596
  363.0 13.8 %copy-start.42 = (f32[2,2,1024]{2,1,0:T(2,128)S(1)}, f32[2,2,1024]{2,1,0:T(2,128)}, u32[]{:S(2)}) copy-start(f32[2,2,1024]{2,1,0:T(2,128)} %copy-done.41) | copy-start | bytes 49156
  404.5 8.8 copy-start.64
  404.5 8.8 copy-start.65
  404.5 8.8 copy-start.66
  404.5 8.8 copy-start.69
  404.5 8.8 copy-start.70
  404.5 9.9 copy-start.76
  404.6 12.2 %copy-start.13 = (f32[2,256,512]{2,1,0:T(8,128)S(1)}, f32[2,256,512]{2,1,0:T(8,128)}, u32[]{:S(2)}) copy-start(f32[2,256,512]{2,1,0:T(8,128)} %copy-done.11) | copy-start | bytes 3145732
  404.6 12.2 %copy-start.61 = (f32[1,512]{1,0:T(1,128)S(1)}, f32[1,512]{1,0:T(1,128)}, u32[]{:S(2)}) copy-start(f32[1,512]{1,0:T(1,128)} %copy-done.60) | copy-start | bytes 6148
  409.7 23.6 %all-to-all-start.7 = ((bf16[2,1024,1,384]{3,0,2,1:T(2,128)(2,1)}), bf16[2,1024,1,384]{3,0,2,1:T(2,128)(2,1)S(1)}, u32[]{:S(2)}, u32[]{:S(2)}) async-start(bf16[2,1024,1,384]{3,0,2,1:T(2,128)(2,1)} %copy.187), calls=%async_computation.7 | async-start | bytes 3145728 | tf_op jit(solution)/shard_map/all_to_all | solution.py:243
  413.2 509.0 %reduce-scatter.16.cloned.1.call-start = ((), (), s32[]{:S(2)}) async-start(), calls=%async_computation.16 | async-start | bytes 294912
  414.3 571.9 %reduce-scatter.18.cloned.1.call-start = ((), (), s32[]{:S(2)}) async-start(), calls=%async_computation.17 | async-start | bytes 294912
  416.5 615.2 %all-reduce.6.cloned.1.call-start = ((), (), s32[]{:S(2)}) async-start(), calls=%async_computation.18 | async-start | bytes 3145728 | tf_op jit(solution)/shard_map/psum | solution.py:274
  754.0 239.9 %copy-start.3 = (f32[2,256,512]{2,1,0:T(8,128)S(1)}, f32[2,256,512]{2,1,0:T(8,128)}, u32[]{:S(2)}) copy-start(f32[2,256,512]{2,1,0:T(8,128)} %copy-done.2) | copy-start | bytes 3145732
  754.0 239.9 %copy-start.49 = (f32[2,256]{1,0:T(2,128)S(1)}, f32[2,256]{1,0:T(2,128)}, u32[]{:S(2)}) copy-start(f32[2,256]{1,0:T(2,128)} %copy-done.48) | copy-start | bytes 6148
  754.0 239.9 %copy-start.63 = (f32[2,256]{1,0:T(2,128)S(1)}, f32[2,256]{1,0:T(2,128)}, u32[]{:S(2)}) copy-start(f32[2,256]{1,0:T(2,128)} %copy-done.62) | copy-start | bytes 6148
  1031.8 6.3 copy-start.43
  (25 other events, 47.1 us)
Sparse Core Ops, SparseCore 0:
  343.5 68.7 reduce-scatter.9
  415.8 262.0 reduce-scatter.13
  682.0 176.2 reduce-scatter.11
  862.0 60.1 reduce-scatter.15
  926.0 60.2 reduce-scatter.17
  989.3 42.4 all-reduce.5
where the time goes:
time: 1060 us; the launch traced here: 1050 us
  waiting for transfers between devices  345 us (33%)
  blocking collectives  332 us (31%)
  local copies, waits for them, and re-layouts  136 us (13%)
  matrix products  107 us (10%)
  other arithmetic  83.8 us (8%)
  starting transfers between devices  24.2 us (2%)
  between operations  16.1 us (2%)
    unnamed x1, blocking collectives  303 us
    unnamed x8, waiting for transfers between devices  125 us
    reduce_scatter x1, waiting for transfers between devices, body(): lax.psum_scatter(jnp.stack(up_list), 'dp', scatter_dimension=1, tiled=True)  98.4 us
    dynamic_update_slice x8, local copies, waits for them, and re-layouts, body(): lax.map(partial(attend_forward, scaling=scaling), (head_view, segment, us...  53 us
    all_to_all x2, waiting for transfers between devices, body(): lax.all_to_all(packed_tokens.reshape(slot_count, local_len, groups, -1),...  39.8 us
    psum x1, waiting for transfers between devices, body(): lax.psum(summed[0].astype(jnp.bfloat16), 'head').astype(jnp.float32)  34.1 us
    all_to_all x2, waiting for transfers between devices, body(): lax.all_to_all(grad_packed, 'head', split_axis=1, concat_axis=2, tiled=True)  30.5 us
  transfers between devices with their start and end apart: 12, of which 10 were waited for; matrix products, arithmetic and copies ran while one was open for 9% of the time, Pallas kernels for 0%

commit v1 on v0

v1 whole, which is shorter than its diff:
```python
import math
from functools import partial
from types import SimpleNamespace

import jax
import jax.numpy as jnp
import numpy as np
from jax import lax
from jax.experimental import pallas as pl
from jax.experimental.pallas import tpu as pltpu
from jax.sharding import PartitionSpec as P

HEADS = 8
EPS = 1e-05
NEG = -1e30
LOG2E = 1.4426950408889634
BF = jnp.bfloat16
F32 = jnp.float32
MESH = pl.DeviceIdType.MESH


EVENTS = {
    ("up", 1): [("D", 1)],
    ("out", 1): [("U", 1)],
    (1, 1): [("O", 1)],
    (2, 1): [("D", 1)],
    (3, 1): [("U", 1), ("O", 1)],
    ("down", 0): [("Q", 1), ("D", 1)],
    ("up", 0): [("D", 0), ("U", 1), ("O", 1)],
    ("out", 0): [("U", 0), ("Q", 1)],
    (0, 0): [("O", 0)],
    (1, 0): [("D", 0), ("Q", 1)],
    (2, 0): [("U", 0), ("O", 0)],
    (3, 0): [("D", 0)],
}


def dot(a, b):
    return jnp.dot(a, b, preferred_element_type=F32)


def dot_t(a, b):
    return lax.dot_general(a, b, (((1,), (1,)), ((), ())), preferred_element_type=F32)


def dot_lt(a, b):
    return lax.dot_general(a, b, (((0,), (0,)), ((), ())), preferred_element_type=F32)


def gelu_parts(h):
    t = 1.0 / (1.0 + (0.3275911 * math.sqrt(0.5)) * jnp.abs(h))
    e = jnp.exp2(h * h * (-0.5 * LOG2E))
    poly = 0.5 * 1.061405429
    for a in (-1.453152027, 1.421413741, -0.284496736, 0.254829592):
        poly = poly * t + 0.5 * a
    q = poly * t * e
    phi = jnp.where(h >= 0.0, 1.0 - q, q)
    return h * phi, phi + h * (e * (1.0 / math.sqrt(2.0 * math.pi)))


def split3(v):
    hi = v.astype(BF).astype(F32)
    rest = v - hi
    mid = rest.astype(BF).astype(F32)
    return hi, mid, rest - mid


class Plan:
    def __init__(self, layers, tl, width, ff, nd):
        self.L, self.TL, self.D, self.FF, self.nd = layers, tl, width, ff, nd
        self.T = 2 * tl
        self.nb = nd.bit_length() - 1
        self.r = width // nd // 4
        self.scratch = {}
        self.n_sem = 0

    def add(self, name, shape, dtype):
        self.scratch[name] = pltpu.VMEM(tuple(shape), dtype)

    def sem(self):
        self.n_sem += 1
        return self.n_sem - 1


def axes_of(nb):
    return [("head", 1), ("head", 2)] + [("dp", 1 << b) for b in reversed(range(nb))]


def stages_of(kind, layer, nb):
    d = [("dp", 1 << b) for b in range(nb)]
    c, x = ("head", 1), ("head", 2)
    y, z = d[:1], d[1:]
    return [s for s in ([c], [x] + y, z) if s]


class Chunk:
    def __init__(self, plan, kind, layer):
        self.kind, self.layer, self.plan = kind, layer, plan
        self.name = f"{kind}{layer}"
        nb, r = plan.nb, plan.r
        rows, cols = {
            "U": (r, plan.FF),
            "O": (r, plan.D),
            "Q": (r, 3 * plan.D),
            "D": (plan.D // 4, plan.FF // plan.nd),
        }[kind]
        self.rows, self.cols = rows, cols
        self.axes = axes_of(nb)
        self.stages = stages_of(kind, layer, nb)
        plan.add("G" + self.name, [2] * len(self.axes) + [rows, cols], BF)
        self.out_shape = (cols, rows) if kind == "D" else (rows, cols)
        plan.add("P" + self.name, self.out_shape, BF)
        self.patterns, self.sems = [], []
        left = len(self.axes)
        for s, dims in enumerate(self.stages):
            left -= len(dims)
            pats = [
                [dims[i] for i in range(len(dims)) if m >> i & 1] for m in range(1, 1 << len(dims))
            ]
            self.patterns.append(pats)
            plan.add(f"R{self.name}_{s}", [len(pats)] + [2] * left + [rows, cols], BF)
            self.sems.append([(plan.sem(), plan.sem()) for _ in pats])
        self.last_sems = [(plan.sem(), plan.sem()) for _ in range(3)]
        self.local_sem = plan.sem()
        self.at = 0

    def index(self, env, stage, flipped):
        done = [a for s in self.stages[:stage] for a in s]
        out = []
        for a in self.axes:
            bit = env.bits[a]
            if a in done:
                out.append(bit)
            elif stage < len(self.stages) and a in self.stages[stage]:
                out.append(1 - bit if a in flipped else bit)
            else:
                out.append(slice(None))
        return tuple(out)

    def copies(self, env, stage):
        for i, (pat, (ss, rs)) in enumerate(zip(self.patterns[stage], self.sems[stage])):
            yield pltpu.make_async_remote_copy(
                src_ref=env.ref["G" + self.name].at[self.index(env, stage, pat)],
                dst_ref=env.ref[f"R{self.name}_{stage}"].at[i],
                send_sem=env.sems.at[ss],
                recv_sem=env.sems.at[rs],
                device_id=env.partner(pat),
                device_id_type=MESH,
            )

    def start(self, env, stage):
        for c in self.copies(env, stage):
            c.start()

    def finish(self, env, stage):
        for c in self.copies(env, stage):
            c.wait()
        own = self.index(env, stage, ())
        g = env.ref["G" + self.name]
        got = env.ref[f"R{self.name}_{stage}"]

        def summed(at):
            piece = iter(at)
            here = tuple(next(piece) if isinstance(o, slice) else o for o in own)
            total = g[here].astype(F32)
            for i in range(len(self.patterns[stage])):
                total = total + got[(i, *at)].astype(F32)
            return total

        if stage < len(self.stages) - 1:
            left = sum(isinstance(o, slice) for o in own)
            for at in np.ndindex(*[2] * left):
                piece = iter(at)
                here = tuple(next(piece) if isinstance(o, slice) else o for o in own)
                g[here] = summed(at).astype(BF)
            return
        total = summed(())
        if self.kind == "D":
            total = total.T
        if self.kind == "Q":
            d = self.plan.D
            lo = lax.broadcasted_iota(jnp.int32, (self.rows, 128), 1) < 64
            tiles = []
            for p in range(HEADS // 2):
                q = total[:, 128 * p : 128 * p + 128]
                k0 = pltpu.roll(total[:, d + 256 * p : d + 256 * p + 128], 64, 1)
                k1 = pltpu.roll(total[:, d + 256 * p + 128 : d + 256 * p + 256], 64, 1)
                tiles += [jnp.where(lo, q, k0), jnp.where(lo, k0, q), k1]
            total = jnp.concatenate(tiles, axis=1)
        env.ref["P" + self.name][...] = total.astype(BF)

    def place(self, env):
        out = env.out[self.kind]
        quarter = env.head
        if self.kind == "D":
            return out.at[self.layer, :, pl.ds(pl.multiple_of(quarter * self.rows, self.rows), self.rows)]
        return out.at[self.layer, quarter]

    def spread(self, env):
        src = env.ref["P" + self.name]
        yield pltpu.make_async_copy(src, self.place(env), env.sems.at[self.local_sem])
        pats = ([("head", 1)], [("head", 2)], [("head", 1), ("head", 2)])
        for pat, (ss, rs) in zip(pats, self.last_sems):
            yield pltpu.make_async_remote_copy(
                src_ref=src,
                dst_ref=self.place(env),
                send_sem=env.sems.at[ss],
                recv_sem=env.sems.at[rs],
                device_id=env.partner(pat),
                device_id_type=MESH,
            )

    def advance(self, env):
        n = len(self.stages)
        if self.at > n:
            return
        if self.at > 0:
            self.finish(env, self.at - 1)
        if self.at < n:
            self.start(env, self.at)
        else:
            for c in self.spread(env):
                c.start()
        self.at += 1

    def complete(self, env):
        while self.at <= len(self.stages):
            self.advance(env)
        for c in self.spread(env):
            c.wait()


def make_plan(layers, tl, width, ff, nd):
    plan = Plan(layers, tl, width, ff, nd)
    t, n = plan.T, HEADS
    add = plan.add
    add("x", (t, width), F32)
    add("dual", (t, width), F32)
    add("br", (t, width), F32)
    add("cot", (2, tl, width), BF)
    add("E", (4 * tl, 128), BF)
    add("EQ", (t, 128), BF)
    add("wq", (layers, width, width), BF)
    add("wkv", (layers, width, 2 * width), BF)
    add("wo", (layers, n // 2, 2, 64, width), BF)
    add("wup", (width, ff), BF)
    add("wdown", (ff, width), BF)
    add("low_in", (layers, 2, tl, width), BF)
    add("KV", (layers, n, 4 * tl, 128), BF)
    add("Q", (layers, n // 2, t, 128), BF)
    add("QX", (layers, t, 128), BF)
    add("att", (layers, t, width), BF)
    add("n_attn", (layers, t, width), BF)
    add("RS", (t, 128), F32)
    add("low_mid", (layers, t, width), BF)
    add("n_ffn", (layers, t, width), BF)
    add("act", (t, ff), BF)
    add("gp", (t, ff), BF)
    add("gb", (t, width), BF)
    add("ksend", (n, t, 128), BF)
    add("krecv", (n, t, 128), BF)
    add("gpk", (t, 3 * width), BF)
    add("GB", (16, width), F32)
    nbits = 2 + plan.nb
    add("GBR", (nbits, 16, width), F32)
    plan.chunks = {}
    for layer in reversed(range(layers)):
        for kind in "DUOQ":
            plan.chunks[kind, layer] = Chunk(plan, kind, layer)
    plan.misc = {}
    for name in (
        ["tok_l", "cot_l", "res_l", "gtok_l", "act_s", "gp_s", "act_b", "gp_b", "gb_out"]
        + [f"{w}{l}{i}" for l in range(layers) for w in ("wqkv", "wo0", "wo1", "wup", "wdown") for i in "ab"]
    ):
        plan.misc[name] = plan.sem()
    for name in (
        ["tok_r", "cot_r", "res_r", "gtok_r"]
        + [f"kv{l}{i}" for l in range(layers) for i in range(2)]
        + [f"dkv{l}{h}" for l in range(layers) for h in range(n)]
        + [f"GB{i}" for i in range(nbits)]
    ):
        plan.misc[name] = (plan.sem(), plan.sem())
    return plan


def kernel(plan, names, *refs):
    (tokens, counts, lengths, wqkv, wo, wup, wdown, gain, bias, cot) = refs[:10]
    (o_res, o_gtok, o_q, o_o, o_u, o_d, o_gb, s_act, s_gp) = refs[10:19]
    ref = dict(zip(names, refs[19:-1]))
    sems = refs[-1]
    r = SimpleNamespace(**{k: v for k, v in ref.items()})
    L, T, TL, D, FF, nb = plan.L, plan.T, plan.TL, plan.D, plan.FF, plan.nb
    n_heads = HEADS
    dp, head = lax.axis_index("dp"), lax.axis_index("head")
    core, xc = head % 2, head // 2
    bits = {("head", 1): core, ("head", 2): xc}
    for b in range(nb):
        bits["dp", 1 << b] = (dp // (1 << b)) % 2

    def partner(pat):
        d, h = dp, head
        for axis, bit in pat:
            v = bits[axis, bit]
            if axis == "dp":
                d = d + bit * (1 - 2 * v)
            else:
                h = h + bit * (1 - 2 * v)
        return (d, h)

    env = SimpleNamespace(
        ref=ref,
        sems=sems,
        bits=bits,
        partner=partner,
        head=head,
        out={"Q": o_q, "O": o_o, "U": o_u, "D": o_d},
    )
    CORE, XP = [("head", 1)], [("head", 2)]

    greet = [CORE, XP, CORE + XP]
    for ch in plan.chunks.values():
        for pats in ch.patterns:
            for pat in pats:
                if pat not in greet:
                    greet.append(pat)
    for b in range(nb):
        if [("dp", 1 << b)] not in greet:
            greet.append([("dp", 1 << b)])
    barrier = pltpu.get_barrier_semaphore()
    for pat in greet:
        pl.semaphore_signal(barrier, inc=1, device_id=partner(pat), device_id_type=MESH)

    def local(src, dst, name):
        return pltpu.make_async_copy(src, dst, sems.at[plan.misc[name]])

    def remote(src, dst, name, pat):
        ss, rs = plan.misc[name]
        return pltpu.make_async_remote_copy(
            src_ref=src,
            dst_ref=dst,
            send_sem=sems.at[ss],
            recv_sem=sems.at[rs],
            device_id=partner(pat),
            device_id_type=MESH,
        )

    stage_ref = [r.act, r.gp]
    raw = [
        local(wqkv.at[l], stage_ref[l].at[:, pl.ds(0, 3 * D)], f"wqkv{l}a") for l in range(L)
    ]
    raw[0].start()
    tok_l = local(tokens.at[xc], r.low_in.at[0, xc], "tok_l")
    tok_l.start()
    cot_l = local(cot.at[xc], r.cot.at[xc], "cot_l")
    wos = []
    for l in range(L):
        wos.append(
            [
                local(wo.at[l, :, e], r.wo.at[l, :, 1 - e], f"wo{e}{l}a")
                for e in range(2)
            ]
        )
    ups = [[local(wup.at[l], r.wup, f"wup{l}{i}") for i in "ab"[: L - l]] for l in range(L)]
    downs = [[local(wdown.at[l], r.wdown, f"wdown{l}{i}") for i in "ab"[: L - l]] for l in range(L)]
    pl.semaphore_wait(barrier, len(greet))
    tok_r = remote(tokens.at[1 - xc], r.low_in.at[0, xc], "tok_r", XP)
    tok_r.start()
    for c in raw[1:] + wos[0] + [ups[0][0], downs[0][0]] + sum(wos[1:], []) + [cot_l]:
        c.start()
    cot_r = remote(cot.at[1 - xc], r.cot.at[xc], "cot_r", XP)
    cot_r.start()

    lane = lax.broadcasted_iota(jnp.int32, (TL, 128), 1)
    row = lax.broadcasted_iota(jnp.int32, (TL, 128), 0)
    count = counts[xc]
    several = count == 4
    for j in range(4):
        quarter = core + 2 * j if j < 2 else (1 - core) + 2 * (j - 2)
        limit_one = lengths[xc, 0] - TL * quarter
        limit = jnp.where(several, lengths[xc, quarter], limit_one)
        usable = row < limit
        same = jnp.logical_or(lane == quarter, jnp.logical_not(several))
        ok = jnp.logical_and(usable, same)
        tile = jnp.where(lane < 4, jnp.where(ok, 0.0, NEG), jnp.where(lane < 32, 1.0, 0.0))
        r.E[pl.ds(TL * j, TL), :] = tile.astype(BF)
    for b in range(2):
        tile = jnp.where(lane == core + 2 * b, 1.0, 0.0).astype(BF)
        r.EQ[pl.ds(TL * b, TL), :] = tile
        for l in range(L):
            r.QX[l, pl.ds(TL * b, TL), :] = tile

    low_half = lax.broadcasted_iota(jnp.int32, (D, 128), 1) < 64
    for l in range(L):
        raw[l].wait()

        def sort_pair(p, _, l=l):
            cols = lambda i: pl.ds(pl.multiple_of(p * 384 + 128 * i, 128), 128)
            t0 = stage_ref[l][:, cols(0)].astype(F32)
            t1 = stage_ref[l][:, cols(1)].astype(F32)
            t2 = stage_ref[l][:, cols(2)].astype(F32)
            r0, r1, r2 = (pltpu.roll(t, 64, 1) for t in (t0, t1, t2))
            r.wq[l, :, pl.ds(pl.multiple_of(p * 128, 128), 128)] = jnp.where(low_half, t0, t1).astype(BF)
            r.wkv[l, :, pl.ds(pl.multiple_of(p * 256, 128), 128)] = jnp.where(low_half, r0, r1).astype(BF)
            r.wkv[l, :, pl.ds(pl.multiple_of(p * 256 + 128, 128), 128)] = r2.astype(BF)
            return 0

        lax.fori_loop(0, n_heads // 2, sort_pair, 0)

    lane1 = lax.broadcasted_iota(jnp.int32, (1, 128), 1)
    m_lo = jnp.where(lane1 < 64, 1.0, 0.0).astype(BF)
    m_hi = jnp.where(lane1 < 64, 0.0, 1.0).astype(BF)
    m_of = [m_lo, m_hi]
    CH = 64

    def rows_of(i):
        return pl.ds(pl.multiple_of(i * CH, CH), CH)

    def normalise(v):
        mu = jnp.mean(v, axis=1, keepdims=True)
        cen = v - mu
        var = jnp.mean(cen * cen, axis=1, keepdims=True)
        rs = lax.rsqrt(var + EPS)
        return cen * rs, rs

    def norm_back(g, n, rs, gain_row):
        h = g * gain_row
        return rs * (
            h - jnp.mean(h, axis=1, keepdims=True) - n * jnp.mean(h * n, axis=1, keepdims=True)
        )

    def keep_rs(col, rows, rs):
        lanes = lax.broadcasted_iota(jnp.int32, (CH, 128), 1)
        r.RS[rows, :] = jnp.where(lanes == col, rs, r.RS[rows, :])

    def fold(v):
        return jnp.sum(v.reshape(CH // 8, 8, D), axis=0)

    r.RS[...] = jnp.zeros((T, 128), F32)
    tok_l.wait()
    tok_r.wait()
    for b in range(2):
        v = r.low_in[0, b].astype(F32)
        r.x[pl.ds(TL * b, TL), :] = v
        r.dual[pl.ds(TL * b, TL), :] = v

    hold = {}

    def forward(l):
        if l > 0:
            r.low_in[l] = r.x[...].astype(BF).reshape(2, TL, D)
        low = r.low_in[l].reshape(T, D)
        sends = []
        hh = n_heads // 2
        for half in range(2):
            kv = dot(low, r.wkv[l, :, D * half : D * half + D]).astype(BF)
            for i in range(hh):
                r.KV[l, half * hh + i, 0:T, :] = kv[:, 128 * i : 128 * i + 128]
            c = remote(
                r.KV.at[l, pl.ds(half * hh, hh), pl.ds(0, T)],
                r.KV.at[l, pl.ds(half * hh, hh), pl.ds(T, T)],
                f"kv{l}{half}",
                CORE,
            )
            c.start()
            sends.append(c)
        q = (dot(low, r.wq[l]) * (LOG2E / 8.0)).astype(BF)
        for p in range(n_heads // 2):
            r.Q[l, p] = q[:, 128 * p : 128 * p + 128]
        sends[0].wait()
        sends[1].wait()
        lane_t = lax.broadcasted_iota(jnp.int32, (TL, 128), 1)

        def attend(p, _):
            outs = []
            for e in range(2):
                h = 2 * p + e
                kve = jnp.concatenate([r.KV[l, h], r.E[...]], axis=1)
                for b in range(2):
                    rows = pl.ds(TL * b, TL)
                    eq = r.EQ[rows, :]
                    qe = jnp.concatenate([r.Q[l, p, rows, :] * m_of[e], eq], axis=1)
                    s = dot_t(qe, kve)
                    top = jnp.max(s, axis=1, keepdims=True)
                    pe = jnp.exp2(s - top).astype(BF)
                    o = dot(pe, kve)
                    total = o[:, 132:133]
                    lse = top + jnp.log(total) * LOG2E
                    outs.append(o[:, :128] * (1.0 / total))
                    hi, mid, lo = split3(-lse)
                    at = lane_t - (8 + 3 * h)
                    old = r.QX[l, rows, :].astype(F32)
                    tile = jnp.where(at == 0, hi, jnp.where(at == 1, mid, jnp.where(at == 2, lo, old)))
                    r.QX[l, rows, :] = tile.astype(BF)
            sel = lane_t < 64
            for b in range(2):
                r.att[l, pl.ds(TL * b, TL), pl.ds(pl.multiple_of(p * 128, 128), 128)] = jnp.where(
                    sel, outs[2 + b], outs[b]
                ).astype(BF)
            return 0

        lax.fori_loop(0, n_heads // 2, attend, 0)
        if l == 0:
            for l2 in range(L):
                for c in wos[l2]:
                    c.wait()
        r.br[...] = dot(r.att[l], r.wo[l].reshape(D, D))

        def after_attn(i, _):
            rows = rows_of(i)
            br = r.br[rows, :]
            r.dual[rows, :] = r.dual[rows, :] + br
            n, rs = normalise(r.x[rows, :] + br)
            r.n_attn[l, rows, :] = n.astype(BF)
            keep_rs(2 * l, rows, rs)
            y = n * gain[2 * l : 2 * l + 1, :] + bias[2 * l : 2 * l + 1, :]
            r.x[rows, :] = y
            r.low_mid[l, rows, :] = y.astype(BF)
            return 0

        lax.fori_loop(0, T // CH, after_attn, 0)
        ups[l][0].wait()
        downs[l][0].wait()
        if l > 0:
            hold["act_s"].wait()
            hold["gp_s"].wait()
        low = r.low_mid[l]
        fb = 512

        def ffn_cols(j, _):
            cols = pl.ds(pl.multiple_of(j * fb, fb), fb)
            a, gp = gelu_parts(dot(r.low_mid[l], r.wup[:, cols]))
            r.act[:, cols] = a.astype(BF)
            r.gp[:, cols] = gp.astype(BF)
            return 0

        lax.fori_loop(0, FF // fb, ffn_cols, 0)
        r.br[...] = dot(r.act[...], r.wdown[...])
        if l < L - 1:
            hold["act_s"] = local(r.act, s_act.at[l], "act_s")
            hold["gp_s"] = local(r.gp, s_gp.at[l], "gp_s")
            hold["act_s"].start()
            hold["gp_s"].start()
            ups[l + 1][0].start()
            downs[l + 1][0].start()

        def after_ffn(i, _):
            rows = rows_of(i)
            br = r.br[rows, :]
            r.dual[rows, :] = r.dual[rows, :] + br
            n, rs = normalise(r.x[rows, :] + br)
            r.n_ffn[l, rows, :] = n.astype(BF)
            keep_rs(2 * l + 1, rows, rs)
            r.x[rows, :] = n * gain[2 * l + 1 : 2 * l + 2, :] + bias[2 * l + 1 : 2 * l + 2, :]
            return 0

        lax.fori_loop(0, T // CH, after_ffn, 0)

    for l in range(L):
        forward(l)

    cot_l.wait()
    cot_r.wait()
    k = 2 * L
    zero = jnp.zeros((8, D), F32)
    r.GB[...] = jnp.zeros((16, D), F32)

    def put_gb(row, acc):
        r.GB[row : row + 1, :] = jnp.sum(acc[0], axis=0, keepdims=True)
        r.GB[8 + row : 9 + row, :] = jnp.sum(acc[1], axis=0, keepdims=True)

    for b in range(2):

        def ending(i, acc, b=b):
            rows = pl.ds(pl.multiple_of(TL * b + i * CH, CH), CH)
            part = pl.ds(pl.multiple_of(i * CH, CH), CH)
            n, rs = normalise(r.dual[rows, :])
            res = r.x[rows, :] + n * gain[k : k + 1, :] + bias[k : k + 1, :]
            g = r.cot[b, part, :].astype(F32)
            r.cot[b, part, :] = res.astype(BF)
            r.x[rows, :] = g
            r.dual[rows, :] = norm_back(g, n, rs, gain[k : k + 1, :])
            return acc[0] + fold(g * n), acc[1] + fold(g)

        acc = lax.fori_loop(0, TL // CH, ending, (zero, zero) if b == 0 else acc)
    put_gb(k, acc)
    res_l = local(r.cot.at[xc], o_res.at[xc], "res_l")
    res_r = remote(r.cot.at[1 - xc], o_res.at[xc], "res_r", XP)
    res_l.start()
    res_r.start()

    def norm_pull(row, n_ref, l):
        def step(i, acc):
            rows = rows_of(i)
            g, n = r.x[rows, :], n_ref[l, rows, :].astype(F32)
            pre = norm_back(g, n, r.RS[rows, row : row + 1], gain[row : row + 1, :])
            r.x[rows, :] = pre
            r.gb[rows, :] = (pre + r.dual[rows, :]).astype(BF)
            return acc[0] + fold(g * n), acc[1] + fold(g)

        put_gb(row, lax.fori_loop(0, T // CH, step, (zero, zero)))

    def store_rows(ch, res, cols, swap=False):
        g = ref["G" + ch.name]
        rr = plan.r
        piece = min(rr, 64)
        for d in range(plan.nd):
            for q in range(4):
                for s in range(0, rr, piece):
                    src = (4 * d + q) * rr + s
                    if swap:
                        src = src ^ 64
                    idx = (q % 2, q // 2) + tuple((d >> b) & 1 for b in reversed(range(nb)))
                    g[idx + (slice(s, s + piece), cols)] = res[src : src + piece].astype(BF)

    def exchange_gb(i):
        pat = ([CORE, XP] + [[("dp", 1 << b)] for b in range(nb)])[i]
        return remote(r.GB, r.GBR.at[i], f"GB{i}", pat)

    order = list(plan.chunks.values())

    def step_chunks(point, l):
        for c in EVENTS.get((point, l), ()):
            plan.chunks[c].advance(env)

    def backward_ffn(l):
        norm_pull(2 * l + 1, r.n_ffn, l)
        if l < L - 1:
            for c in (hold["act_b"], hold["gp_b"], ups[l][1], downs[l][1]):
                c.wait()
        ch = plan.chunks["D", l]
        gbt = r.gb[...].astype(F32).T.astype(BF)
        dcols = ch.cols
        g = ref["G" + ch.name]
        for d in range(plan.nd):
            idx = tuple((d >> b) & 1 for b in reversed(range(nb)))
            step = min(dcols, 512)
            for s in range(0, dcols, step):
                res = dot(gbt, r.act[:, d * dcols + s : d * dcols + s + step])
                for q in range(4):
                    g[(q % 2, q // 2) + idx + (slice(None), slice(s, s + step))] = res[
                        q * ch.rows : (q + 1) * ch.rows
                    ].astype(BF)
        ch.advance(env)
        step_chunks("down", l)
        fb = 512

        def hidden_cols(j, _):
            cols = pl.ds(pl.multiple_of(j * fb, fb), fb)
            gact = dot_t(r.gb[...], r.wdown[cols, :])
            r.gp[:, cols] = (gact * r.gp[:, cols].astype(F32)).astype(BF)
            return 0

        lax.fori_loop(0, FF // fb, hidden_cols, 0)
        ch = plan.chunks["U", l]
        lmt = r.low_mid[l].astype(F32).T.astype(BF)
        for j in range(FF // fb):
            res = dot(lmt, r.gp[:, j * fb : (j + 1) * fb])
            store_rows(ch, res, slice(j * fb, (j + 1) * fb))
        ch.advance(env)
        step_chunks("up", l)
        r.br[...] = dot_t(r.gp[...], r.wup[...])
        r.x[...] = r.x[...] + r.br[...]
        if l > 0:
            hold["act_b"] = local(s_act.at[l - 1], r.act, "act_b")
            hold["gp_b"] = local(s_gp.at[l - 1], r.gp, "gp_b")
            for c in (hold["act_b"], hold["gp_b"], ups[l - 1][1], downs[l - 1][1]):
                c.start()

    def backward_attn(l):
        norm_pull(2 * l, r.n_attn, l)
        ch = plan.chunks["O", l]
        res = dot(r.att[l].astype(F32).T.astype(BF), r.gb[...])
        store_rows(ch, res, slice(None), swap=True)
        ch.advance(env)
        step_chunks("out", l)
        r.gb[...] = dot_t(r.gb[...], r.wo[l].reshape(D, D)).astype(BF)
        lane_t = lax.broadcasted_iota(jnp.int32, (T, 128), 1)
        scale = [
            jnp.where(lane1 < 64, 1.0 / LOG2E, 1.0),
            jnp.where(lane1 < 64, 1.0, 1.0 / LOG2E),
        ]

        def dkv_copy(h, name_h):
            ss, rs = plan.misc[f"dkv{l}0"]
            return pltpu.make_async_remote_copy(
                src_ref=r.ksend.at[h],
                dst_ref=r.krecv.at[h],
                send_sem=sems.at[ss + 2 * h],
                recv_sem=sems.at[rs + 2 * h],
                device_id=partner(CORE),
                device_id_type=MESH,
            )

        def pair(p, _):
            tile = pl.ds(pl.multiple_of(p * 128, 128), 128)
            att = r.att[l, :, tile].astype(F32)
            dqts = []
            for e in range(2):
                h = 2 * p + e
                q = r.Q[l, p] * m_of[e]
                at = lane1 - (8 + 3 * h)
                mine = jnp.where(
                    jnp.logical_or(lane1 < 4, jnp.logical_and(at >= 0, at < 3)), 1.0, 0.0
                ).astype(BF)
                do = r.gb[:, tile] * m_of[1 - e]
                centre = jnp.sum(att * do.astype(F32), axis=1, keepdims=True)
                hi, mid, lo = split3(-centre)
                ed = jnp.where(
                    lane_t == 4, hi, jnp.where(lane_t == 5, mid, jnp.where(lane_t == 6, lo, 0.0))
                ).astype(BF)
                qd = jnp.concatenate(
                    [
                        jnp.concatenate([q, r.QX[l] * mine], axis=1),
                        jnp.concatenate([do, ed], axis=1),
                    ],
                    axis=0,
                )
                dq_in = jnp.concatenate([do, q], axis=0)
                dqt = None
                for j in (2, 3, 0, 1):
                    rows = pl.ds(TL * j, TL)
                    kv = r.KV[l, h, rows, :]
                    ss = dot_t(jnp.concatenate([kv, r.E[rows, :]], axis=1), qd)
                    pr = jnp.exp2(ss[:, :T])
                    ds = (pr * ss[:, T:]).astype(BF)
                    dkv = dot(jnp.concatenate([pr.astype(BF), ds], axis=1), dq_in) * scale[e]
                    part = dot_lt(kv, ds)
                    dqt = part if dqt is None else dqt + part
                    if j >= 2:
                        r.ksend[h, pl.ds(TL * (j - 2), TL), :] = dkv.astype(BF)
                    else:
                        r.gpk[rows, pl.ds(pl.multiple_of(D + h * 128, 128), 128)] = dkv.astype(BF)
                    if j == 3:
                        dkv_copy(h, None).start()
                dqts.append(dqt)
            dq = jnp.concatenate([dqts[0][:64], dqts[1][64:]], axis=0).T * (1.0 / 8.0)
            r.gpk[:, tile] = dq.astype(BF)
            for at in range(n_heads // 2):
                if (at, l) in EVENTS:

                    @pl.when(p == at)
                    def _(at=at):
                        step_chunks(at, l)

            return 0

        lax.fori_loop(0, n_heads // 2, pair, 0)
        for h in range(n_heads):
            dkv_copy(h, None).wait()
            cols = slice(D + 128 * h, D + 128 * h + 128)
            r.gpk[:, cols] = (r.gpk[:, cols].astype(F32) + r.krecv[h].astype(F32)).astype(BF)
        ch = plan.chunks["Q", l]
        lit = r.low_in[l].reshape(T, D).astype(F32).T.astype(BF)
        for j in range(3):
            cols = slice(j * D, (j + 1) * D)
            store_rows(ch, dot(lit, r.gpk[:, cols]), cols)
        ch.advance(env)
        r.br[...] = dot_t(r.gpk[:, :D], r.wq[l]) + dot_t(r.gpk[:, D:], r.wkv[l])
        r.x[...] = r.x[...] + r.br[...]

    for l in reversed(range(L)):
        backward_ffn(l)
        backward_attn(l)

    res_l.wait()
    res_r.wait()
    for b in range(2):
        rows = pl.ds(TL * b, TL)
        r.cot[b] = (r.x[rows, :] + r.dual[rows, :]).astype(BF)
    gt_l = local(r.cot.at[xc], o_gtok.at[xc], "gtok_l")
    gt_r = remote(r.cot.at[1 - xc], o_gtok.at[xc], "gtok_r", XP)
    gt_l.start()
    gt_r.start()
    for i in range(2 + nb):
        c = exchange_gb(i)
        c.start()
        c.wait()
        r.GB[...] = r.GB[...] + r.GBR[i]
    gb_out = local(r.GB, o_gb, "gb_out")
    gb_out.start()
    for ch in order:
        ch.complete(env)
    gb_out.wait()
    gt_l.wait()
    gt_r.wait()


def body(nd, tokens, counts, lengths, wqkv, wo, wup, wdown, gain, bias, cot):
    layers, width = wo.shape[0], wo.shape[2]
    ff = wup.shape[2]
    tl = tokens.shape[1]
    plan = make_plan(layers, tl, width, ff, nd)
    names = list(plan.scratch)
    any_spec = pl.BlockSpec(memory_space=pl.ANY)
    vmem = pl.BlockSpec(memory_space=pltpu.VMEM)
    smem = pl.BlockSpec(memory_space=pltpu.SMEM)
    rr = plan.r
    sd = jax.ShapeDtypeStruct
    outs = pl.pallas_call(
        partial(kernel, plan, names),
        out_shape=(
            sd(tokens.shape, BF),
            sd(tokens.shape, BF),
            sd((layers, 4, rr, 3 * width), BF),
            sd((layers, 4, rr, width), BF),
            sd((layers, 4, rr, ff), BF),
            sd((layers, ff // nd, width), BF),
            sd((16, width), F32),
            sd((max(layers - 1, 1), 2 * tl, ff), BF),
            sd((max(layers - 1, 1), 2 * tl, ff), BF),
        ),
        in_specs=[any_spec, smem, smem, any_spec, any_spec, any_spec, any_spec, vmem, vmem, any_spec],
        out_specs=[any_spec] * 9,
        scratch_shapes=[plan.scratch[k] for k in names] + [pltpu.SemaphoreType.DMA((plan.n_sem,))],
        compiler_params=pltpu.CompilerParams(
            collective_id=0, has_side_effects=True, vmem_limit_bytes=60 * 2**20
        ),
    )(
        tokens,
        counts,
        lengths,
        wqkv,
        wo.reshape(layers, HEADS // 2, 2, 64, width),
        wup,
        wdown,
        gain,
        bias,
        cot,
    )
    res, gtok, gq, go, gu, gd, gb = outs[:7]
    result = res.astype(F32)
    grad_tokens = gtok.astype(F32)
    grads = [
        gq.astype(F32).reshape(layers, 4 * rr, 3 * width),
        go.astype(F32).reshape(layers, 4 * rr, width),
        gu.astype(F32).reshape(layers, 4 * rr, ff),
        gd.astype(F32),
    ]
    norms = gain.shape[0]
    gains = [gb[:norms], gb[8 : 8 + norms]]
    size = lax.axis_size("dp")
    if nd == size:
        piece = width // size
        start = lax.axis_index("dp") * piece
        gains = [lax.dynamic_slice(g, (0, start), (norms, piece)) for g in gains]
    else:
        grads = [lax.psum_scatter(g, "dp", scatter_dimension=1, tiled=True) for g in grads]
        gains = [lax.psum_scatter(g, "dp", scatter_dimension=1, tiled=True) for g in gains]
    return (result, grad_tokens, *grads, *gains)


def solution(mesh):
    dp = mesh.shape["dp"]
    nd = dp if dp & (dp - 1) == 0 and 512 % (64 * dp) == 0 else 1
    return jax.shard_map(
        partial(body, nd),
        mesh=mesh,
        in_specs=(
            P("dp", "head", None),
            P("dp"),
            P("dp", None),
            P(),
            P(),
            P(),
            P(),
            P(),
            P(),
            P("dp", "head", None),
        ),
        out_specs=(
            P("dp", "head", None),
            P("dp", "head", None),
            P(None, "dp", None),
            P(None, "dp", None),
            P(None, "dp", None),
            P(None, "dp", None),
            P(None, "dp"),
            P(None, "dp"),
        ),
        check_vma=False,
    )
```

time: 1060 us -> 201 us (0.19); the launches traced: 1050 us -> 201 us
  waiting for transfers between devices: 345 us -> 0 us
  blocking collectives: 332 us -> 0 us
  Pallas kernels: 0 us -> 191 us
  local copies, waits for them, and re-layouts: 136 us -> 1.51 us
  matrix products: 107 us -> 0 us
  other arithmetic: 83.8 us -> 8.27 us
  starting transfers between devices: 24.2 us -> 0 us
  between operations: 16.1 us -> 0.67 us
    unnamed x1 -> x0, blocking collectives: 303 us -> none
    pallas_call x0 -> x1, Pallas kernels: none -> 191 us  [body(): pl.pallas_call(partial(kernel, plan, names), out_shape=(sd(tokens.shape,...]
    unnamed x8 -> x0, waiting for transfers between devices: 125 us -> none
    dot_general x52 -> x0, matrix products: 107 us -> none  [the longest x8 12.8 us: masked_scores(): jnp.einsum('qhd,khd->hqk', query_rows, key_rows, preferred_element_type=j...]
    reduce_scatter x3 -> x0, waiting for transfers between devices: 98.4 us -> none  [the longest x1 98.4 us: body(): lax.psum_scatter(jnp.stack(up_list), 'dp', scatter_dimension=1, tiled=True)]
    all_to_all x6 -> x0, waiting for transfers between devices: 87.8 us -> none  [the longest x2 39.8 us: body(): lax.all_to_all(packed_tokens.reshape(slot_count, local_len, groups, -1),...]
    dynamic_update_slice x8 -> x0, local copies, waits for them, and re-layouts: 53 us -> none  [body(): lax.map(partial(attend_forward, scaling=scaling), (head_view, segment, us...]
    convert_element_type x18 -> x3, other arithmetic: 45.1 us -> 4.38 us  [the longest x1 2.18 us: body(): result = res.astype(F32)]
  transfers between devices with their start and end apart: 12 -> 0, of which waited for: 10 -> 0; matrix products, arithmetic and copies ran while one was open for 9% -> 0% of each run, Pallas kernels for 0% -> 0%
where the time goes in v1:
time: 201 us
  Pallas kernels  191 us (95%)
  other arithmetic  8.27 us (4%)
    pallas_call x1, Pallas kernels, body(): pl.pallas_call(partial(kernel, plan, names), out_shape=(sd(tokens.shape,...  191 us

profile of v1, /device:TPU:0, one launch (start us, length us, event | category | flops | bytes accessed | tf_op | source)
XLA Modules:
  0.0 201.2 jit_solution(11289952019305978374)
XLA Ops:
  0.6 190.8 %shard_map.161 = (bf16[2,256,512]{2,1,0:T(8,128)(2,1)}, bf16[2,256,512]{2,1,0:T(8,128)(2,1)}, bf16[2,4,16,1536]{3,2,1,0:T(8,128)(2,1)}, bf16[2,4,16,512]{3,2,1,0...) custom-call(bf16[2,256,512]{2,1,0:T(8,128)(2,1)} %refs_0_.1, ...), custom_call_target="tpu_custom_call" | custom-call | tf_op jit(solution)/shard_map/pallas_call | solution.py:799
  191.4 0.0 copy-start.1
  191.4 0.0 copy-start
  191.4 0.8 fusion
  192.2 0.7 constant_dynamic-slice_fusion
  192.9 0.0 copy-start.2
  192.9 2.2 %bitcast_convert_fusion = f32[2,64,2048]{2,1,0:T(8,128)} fusion(bf16[2,4,16,2048]{3,2,1,0:T(8,128)(2,1)} %get-tuple-element.19), kind=kLoop, calls=%fused_computation | loop fusion | flops 262144 | bytes 1572864 | tf_op jit(solution)/shard_map/reshape | solution.py:836
  195.1 0.0 copy-start.3
  195.1 2.2 %convert_element_type.12 = f32[2,256,512]{2,1,0:T(8,128)} convert(bf16[2,256,512]{2,1,0:T(8,128)(2,1)} %get-tuple-element.15) | non-fusion elementwise | flops 262144 | bytes 1572864 | tf_op jit(solution)/shard_map/convert_element_type | solution.py:831
  197.3 0.0 copy-done.1
  197.3 1.1 convert_element_type.13
  198.4 0.0 copy-done
  198.4 1.1 convert_element_type.14
  199.5 0.0 copy-done.2
  199.5 1.0 bitcast_convert_fusion.1
  200.5 0.0 copy-done.3
  200.5 0.7 bitcast_convert_fusion.2
Async XLA Ops:
  191.4 5.9 %copy-start.1 = (bf16[2,256,512]{2,1,0:T(8,128)(2,1)S(1)}, bf16[2,256,512]{2,1,0:T(8,128)(2,1)}, u32[]{:S(2)}) copy-start(bf16[2,256,512]{2,1,0:T(8,128)(2,1)} %get-tuple-element.16) | copy-start | bytes 1572868
  191.4 7.0 %copy-start = (bf16[2,256,512]{2,1,0:T(8,128)(2,1)S(1)}, bf16[2,256,512]{2,1,0:T(8,128)(2,1)}, u32[]{:S(2)}) copy-start(bf16[2,256,512]{2,1,0:T(8,128)(2,1)} %get-tuple-element.20) | copy-start | bytes 1572868
  192.9 6.6 %copy-start.2 = (bf16[2,4,16,1536]{3,2,1,0:T(8,128)(2,1)S(1)}, bf16[2,4,16,1536]{3,2,1,0:T(8,128)(2,1)}, u32[]{:S(2)}) copy-start(bf16[2,4,16,1536]{3,2,1,0:T(8,128)(2,1)} %get-tuple-element.17) | copy-start | bytes 1179652
  195.1 5.4 %copy-start.3 = (bf16[2,4,16,512]{3,2,1,0:T(8,128)(2,1)S(1)}, bf16[2,4,16,512]{3,2,1,0:T(8,128)(2,1)}, u32[]{:S(2)}) copy-start(bf16[2,4,16,512]{3,2,1,0:T(8,128)(2,1)} %get-tuple-element.18) | copy-start | bytes 393220
